TPU v7x, 256 devices: a whole 4x4x8 slice. The times are simulated.
256 devices in a mesh: gx: 8 (over z), gy: 16 (over x, y), gz: 2 (over core).
Axes of the slice: x: 4, y: 4, z: 8, core: 2. Of those that a mesh axis runs over, the one named last changes fastest.
Arguments:
- features: bfloat16 [64, 2097152], P(None, ('gx', 'gy', 'gz')), may hold values from -6 to 6
- grad_out: bfloat16 [64, 2097152], P(None, ('gx', 'gy', 'gz')), may hold values from -6 to 6
- weights: bfloat16 [27, 64, 64], replicated, may hold values from -0.15625 to 0.15625
- neighbor_map: int32 [27, 2097152], P(None, ('gx', 'gy', 'gz')), may hold values from 0 to 13824, as said below
- send_list: int32 [1441792], P(('gx', 'gy', 'gz')), may hold values from 0 to 8192, as said below
Outputs:
- grad_in: bfloat16 [64, 2097152], P(None, ('gx', 'gy', 'gz'))
- grad_weights: float32 [27, 64, 64], replicated
Inputs may be any that keep to these rules, and one draw needn't show every extreme that they name: `neighbor_map`: for each offset and slot: a value below 8192 is a slot of the same block, 8192 to 13823 a column of the block's halo table, 13824 none. The middle offset 27 // 2 maps every used slot to itself; unused slots map to none at every offset. `send_list`: each entry is a used voxel slot of the sending block, or 8192 for an empty entry; at least half of every direction's entries are used, and one owner fills all of them.
All inputs are finite; a program needn't handle non-finite values.
Results may differ from a plain program's by a relative error of at most 0.001.
Values may be sent and summed in bfloat16 or wider, within the bound.
A program may use at most 64 MiB of HBM per device.

v0:
```python
import math

import jax
import jax.numpy as jnp
from jax import lax
from jax.sharding import PartitionSpec as P

FACE_CAP = 512
EDGE_CAP = 128
CORNER_CAP = 128


def shifted(shard, axis, by):
    count = lax.axis_size(axis)
    pairs = [(i, i + by) for i in range(count) if 0 <= i + by < count]
    return lax.ppermute(shard, axis, pairs)


def transfer_headings():
    found_list = []
    for kernel_weight in (1, 2, 3):
        for step_x in (-1, 0, 1):
            for step_y in (-1, 0, 1):
                for depth_step in (-1, 0, 1):
                    if abs(step_x) + abs(step_y) + abs(depth_step) == kernel_weight:
                        found_list.append((step_x, step_y, depth_step))
    return found_list


def block_room_limits():
    result_list = []
    for stencil_displacement in transfer_headings():
        nonzero = (
            abs(stencil_displacement[0])
            + abs(stencil_displacement[1])
            + abs(stencil_displacement[2])
        )
        if nonzero == 1:
            result_list.append(FACE_CAP)
        elif nonzero == 2:
            result_list.append(EDGE_CAP)
        else:
            result_list.append(CORNER_CAP)
    return result_list


def neighbor_move(block, axis_pos, amount):
    if axis_pos == 0:
        return shifted(block, "gx", amount)
    if axis_pos == 1:
        return shifted(block, "gy", amount)
    return shifted(block, "gz", amount)


def per_device(features, grad_out, weights, neighbor_map, send_list):
    channels, slot_count = grad_out.shape
    grad_rows = grad_out.T
    zero_row = jnp.zeros((1, channels), grad_out.dtype)
    padded = jnp.concatenate([grad_rows, zero_row], axis=0)
    outgoing = jnp.take(padded, send_list, axis=0)
    offsets_all = transfer_headings()
    pieces = []
    start_row = 0
    for place_room_limit in block_room_limits():
        pieces.append(outgoing[start_row : start_row + place_room_limit])
        start_row += place_room_limit
    for position in range(len(pieces)):
        for axis_pos in range(3):
            amount = offsets_all[position][axis_pos]
            if amount != 0:
                pieces[position] = neighbor_move(pieces[position], axis_pos, amount)
    lookup_rows = jnp.concatenate([grad_rows] + pieces + [zero_row], axis=0)

    def accumulate(running, parts):
        kernel, indices = parts
        picked = jnp.take(lookup_rows, indices, axis=0)
        running = running + lax.dot_general(
            kernel, picked, (((1,), (1,)), ((), ())), preferred_element_type=jnp.float32
        )
        partial_w = jnp.dot(features, picked, preferred_element_type=jnp.float32)
        return (running, partial_w)

    start_sum = jnp.zeros((channels, slot_count), jnp.float32)
    summed, partial_weights = lax.scan(accumulate, start_sum, (weights, neighbor_map))
    grad_in = summed.astype(jnp.bfloat16)
    devices_all = lax.axis_size("gx") * lax.axis_size("gy") * lax.axis_size("gz")
    scale_factor = 1.0 / math.sqrt(slot_count * devices_all)
    grad_weights = lax.psum(partial_weights, ("gx", "gy", "gz")) * scale_factor
    return (grad_in, grad_weights)


def solution(mesh):
    placed = (
        P(None, ("gx", "gy", "gz")),
        P(None, ("gx", "gy", "gz")),
        P(),
        P(None, ("gx", "gy", "gz")),
        P(("gx", "gy", "gz")),
    )
    return jax.shard_map(
        per_device,
        mesh=mesh,
        in_specs=placed,
        out_specs=(P(None, ("gx", "gy", "gz")), P()),
        check_vma=False,
    )
```

profile of v0, /device:TPU:1, one launch (start us, length us, event | category | flops | bytes accessed | tf_op | source)
XLA Modules:
  0.0 1662.5 jit_solution(11823807202035280383)
XLA Ops:
  13.8 12.2 gather_fusion.1
  32.4 5.8 collective-permute-start.2
  39.5 4.9 collective-permute-start.4
  66.8 5.4 collective-permute-start.9
  79.1 5.6 collective-permute-start.13
  84.7 6.2 collective-permute-start.22
  99.8 4.6 collective-permute-start.26
  107.7 4.9 collective-permute-start.28
  133.0 5.5 collective-permute-start.42
  151.1 4.9 collective-permute-start.51
  156.0 4.9 collective-permute-start.37
  168.7 4.9 collective-permute-start.49
  173.6 5.8 collective-permute-start.52
  194.9 1203.6 %while.13 = (s32[]{:T(128)}, f32[64,8192]{1,0:T(8,128)}, f32[27,64,64]{2,1,0:T(8,128)}, bf16[27,64,64]{2,1,0:T(8,128)(2,1)}, s32[27,8192]{1,0:T(8,128)}, /*index...) while((s32[]{:T(128)}, f32[64,8192]{1,0:T(8,128)}, ...), condition=%wide.region_1.2_spmd.clone, body=%wide.region_0.1_spmd.clone.sunk | while | flops 136396800 | bytes 19260580 | solution.py:84
  197.1 31.9 %gather_fusion = bf16[8192,64]{1,0:T(8,128)(2,1)} fusion(bf16[13825,64]{1,0:T(8,128)(2,1)S(1)} %get-tuple-element.177, s32[8192]{0:T(1024)} %broadcast_clamp_fusion.2), kind=kCustom, calls=%fused_computation.clone.clone.1 | custom fusion | bytes 2129920 | tf_op jit(solution)/shard_map/while/body/eval_jaxpr/jit(_take)/gather | solution.py:76
  241.4 31.9 %gather_fusion = bf16[8192,64]{1,0:T(8,128)(2,1)} fusion(bf16[13825,64]{1,0:T(8,128)(2,1)S(1)} %get-tuple-element.177, s32[8192]{0:T(1024)} %broadcast_clamp_fusion.2), kind=kCustom, calls=%fused_computation.clone.clone.1 | custom fusion | bytes 2129920 | tf_op jit(solution)/shard_map/while/body/eval_jaxpr/jit(_take)/gather | solution.py:76
  286.0 31.9 %gather_fusion = bf16[8192,64]{1,0:T(8,128)(2,1)} fusion(bf16[13825,64]{1,0:T(8,128)(2,1)S(1)} %get-tuple-element.177, s32[8192]{0:T(1024)} %broadcast_clamp_fusion.2), kind=kCustom, calls=%fused_computation.clone.clone.1 | custom fusion | bytes 2129920 | tf_op jit(solution)/shard_map/while/body/eval_jaxpr/jit(_take)/gather | solution.py:76
  330.5 31.9 %gather_fusion = bf16[8192,64]{1,0:T(8,128)(2,1)} fusion(bf16[13825,64]{1,0:T(8,128)(2,1)S(1)} %get-tuple-element.177, s32[8192]{0:T(1024)} %broadcast_clamp_fusion.2), kind=kCustom, calls=%fused_computation.clone.clone.1 | custom fusion | bytes 2129920 | tf_op jit(solution)/shard_map/while/body/eval_jaxpr/jit(_take)/gather | solution.py:76
  363.2 4.3 convolution_add_fusion.2
  375.1 31.9 %gather_fusion = bf16[8192,64]{1,0:T(8,128)(2,1)} fusion(bf16[13825,64]{1,0:T(8,128)(2,1)S(1)} %get-tuple-element.177, s32[8192]{0:T(1024)} %broadcast_clamp_fusion.2), kind=kCustom, calls=%fused_computation.clone.clone.1 | custom fusion | bytes 2129920 | tf_op jit(solution)/shard_map/while/body/eval_jaxpr/jit(_take)/gather | solution.py:76
  407.8 4.3 convolution_add_fusion.2
  419.7 31.9 %gather_fusion = bf16[8192,64]{1,0:T(8,128)(2,1)} fusion(bf16[13825,64]{1,0:T(8,128)(2,1)S(1)} %get-tuple-element.177, s32[8192]{0:T(1024)} %broadcast_clamp_fusion.2), kind=kCustom, calls=%fused_computation.clone.clone.1 | custom fusion | bytes 2129920 | tf_op jit(solution)/shard_map/while/body/eval_jaxpr/jit(_take)/gather | solution.py:76
  452.4 4.3 convolution_add_fusion.2
  464.3 31.9 %gather_fusion = bf16[8192,64]{1,0:T(8,128)(2,1)} fusion(bf16[13825,64]{1,0:T(8,128)(2,1)S(1)} %get-tuple-element.177, s32[8192]{0:T(1024)} %broadcast_clamp_fusion.2), kind=kCustom, calls=%fused_computation.clone.clone.1 | custom fusion | bytes 2129920 | tf_op jit(solution)/shard_map/while/body/eval_jaxpr/jit(_take)/gather | solution.py:76
  497.0 4.3 convolution_add_fusion.2
  508.9 31.9 %gather_fusion = bf16[8192,64]{1,0:T(8,128)(2,1)} fusion(bf16[13825,64]{1,0:T(8,128)(2,1)S(1)} %get-tuple-element.177, s32[8192]{0:T(1024)} %broadcast_clamp_fusion.2), kind=kCustom, calls=%fused_computation.clone.clone.1 | custom fusion | bytes 2129920 | tf_op jit(solution)/shard_map/while/body/eval_jaxpr/jit(_take)/gather | solution.py:76
  541.6 4.3 convolution_add_fusion.2
  553.5 31.9 %gather_fusion = bf16[8192,64]{1,0:T(8,128)(2,1)} fusion(bf16[13825,64]{1,0:T(8,128)(2,1)S(1)} %get-tuple-element.177, s32[8192]{0:T(1024)} %broadcast_clamp_fusion.2), kind=kCustom, calls=%fused_computation.clone.clone.1 | custom fusion | bytes 2129920 | tf_op jit(solution)/shard_map/while/body/eval_jaxpr/jit(_take)/gather | solution.py:76
  586.2 4.3 convolution_add_fusion.2
  598.1 31.9 %gather_fusion = bf16[8192,64]{1,0:T(8,128)(2,1)} fusion(bf16[13825,64]{1,0:T(8,128)(2,1)S(1)} %get-tuple-element.177, s32[8192]{0:T(1024)} %broadcast_clamp_fusion.2), kind=kCustom, calls=%fused_computation.clone.clone.1 | custom fusion | bytes 2129920 | tf_op jit(solution)/shard_map/while/body/eval_jaxpr/jit(_take)/gather | solution.py:76
  630.8 4.3 convolution_add_fusion.2
  642.7 31.9 %gather_fusion = bf16[8192,64]{1,0:T(8,128)(2,1)} fusion(bf16[13825,64]{1,0:T(8,128)(2,1)S(1)} %get-tuple-element.177, s32[8192]{0:T(1024)} %broadcast_clamp_fusion.2), kind=kCustom, calls=%fused_computation.clone.clone.1 | custom fusion | bytes 2129920 | tf_op jit(solution)/shard_map/while/body/eval_jaxpr/jit(_take)/gather | solution.py:76
  675.4 4.3 convolution_add_fusion.2
  687.3 31.9 %gather_fusion = bf16[8192,64]{1,0:T(8,128)(2,1)} fusion(bf16[13825,64]{1,0:T(8,128)(2,1)S(1)} %get-tuple-element.177, s32[8192]{0:T(1024)} %broadcast_clamp_fusion.2), kind=kCustom, calls=%fused_computation.clone.clone.1 | custom fusion | bytes 2129920 | tf_op jit(solution)/shard_map/while/body/eval_jaxpr/jit(_take)/gather | solution.py:76
  719.9 4.3 convolution_add_fusion.2
  731.8 31.9 %gather_fusion = bf16[8192,64]{1,0:T(8,128)(2,1)} fusion(bf16[13825,64]{1,0:T(8,128)(2,1)S(1)} %get-tuple-element.177, s32[8192]{0:T(1024)} %broadcast_clamp_fusion.2), kind=kCustom, calls=%fused_computation.clone.clone.1 | custom fusion | bytes 2129920 | tf_op jit(solution)/shard_map/while/body/eval_jaxpr/jit(_take)/gather | solution.py:76
  764.5 4.3 convolution_add_fusion.2
  776.4 31.9 %gather_fusion = bf16[8192,64]{1,0:T(8,128)(2,1)} fusion(bf16[13825,64]{1,0:T(8,128)(2,1)S(1)} %get-tuple-element.177, s32[8192]{0:T(1024)} %broadcast_clamp_fusion.2), kind=kCustom, calls=%fused_computation.clone.clone.1 | custom fusion | bytes 2129920 | tf_op jit(solution)/shard_map/while/body/eval_jaxpr/jit(_take)/gather | solution.py:76
  809.1 4.3 convolution_add_fusion.2
  821.0 31.9 %gather_fusion = bf16[8192,64]{1,0:T(8,128)(2,1)} fusion(bf16[13825,64]{1,0:T(8,128)(2,1)S(1)} %get-tuple-element.177, s32[8192]{0:T(1024)} %broadcast_clamp_fusion.2), kind=kCustom, calls=%fused_computation.clone.clone.1 | custom fusion | bytes 2129920 | tf_op jit(solution)/shard_map/while/body/eval_jaxpr/jit(_take)/gather | solution.py:76
  853.7 4.3 convolution_add_fusion.2
  865.6 31.9 %gather_fusion = bf16[8192,64]{1,0:T(8,128)(2,1)} fusion(bf16[13825,64]{1,0:T(8,128)(2,1)S(1)} %get-tuple-element.177, s32[8192]{0:T(1024)} %broadcast_clamp_fusion.2), kind=kCustom, calls=%fused_computation.clone.clone.1 | custom fusion | bytes 2129920 | tf_op jit(solution)/shard_map/while/body/eval_jaxpr/jit(_take)/gather | solution.py:76
  898.3 4.3 convolution_add_fusion.2
  910.2 31.9 %gather_fusion = bf16[8192,64]{1,0:T(8,128)(2,1)} fusion(bf16[13825,64]{1,0:T(8,128)(2,1)S(1)} %get-tuple-element.177, s32[8192]{0:T(1024)} %broadcast_clamp_fusion.2), kind=kCustom, calls=%fused_computation.clone.clone.1 | custom fusion | bytes 2129920 | tf_op jit(solution)/shard_map/while/body/eval_jaxpr/jit(_take)/gather | solution.py:76
  942.9 4.3 convolution_add_fusion.2
  954.8 31.9 %gather_fusion = bf16[8192,64]{1,0:T(8,128)(2,1)} fusion(bf16[13825,64]{1,0:T(8,128)(2,1)S(1)} %get-tuple-element.177, s32[8192]{0:T(1024)} %broadcast_clamp_fusion.2), kind=kCustom, calls=%fused_computation.clone.clone.1 | custom fusion | bytes 2129920 | tf_op jit(solution)/shard_map/while/body/eval_jaxpr/jit(_take)/gather | solution.py:76
  987.5 4.3 convolution_add_fusion.2
  999.4 31.9 %gather_fusion = bf16[8192,64]{1,0:T(8,128)(2,1)} fusion(bf16[13825,64]{1,0:T(8,128)(2,1)S(1)} %get-tuple-element.177, s32[8192]{0:T(1024)} %broadcast_clamp_fusion.2), kind=kCustom, calls=%fused_computation.clone.clone.1 | custom fusion | bytes 2129920 | tf_op jit(solution)/shard_map/while/body/eval_jaxpr/jit(_take)/gather | solution.py:76
  1032.1 4.3 convolution_add_fusion.2
  1044.0 31.9 %gather_fusion = bf16[8192,64]{1,0:T(8,128)(2,1)} fusion(bf16[13825,64]{1,0:T(8,128)(2,1)S(1)} %get-tuple-element.177, s32[8192]{0:T(1024)} %broadcast_clamp_fusion.2), kind=kCustom, calls=%fused_computation.clone.clone.1 | custom fusion | bytes 2129920 | tf_op jit(solution)/shard_map/while/body/eval_jaxpr/jit(_take)/gather | solution.py:76
  1076.7 4.3 convolution_add_fusion.2
  1088.6 31.9 %gather_fusion = bf16[8192,64]{1,0:T(8,128)(2,1)} fusion(bf16[13825,64]{1,0:T(8,128)(2,1)S(1)} %get-tuple-element.177, s32[8192]{0:T(1024)} %broadcast_clamp_fusion.2), kind=kCustom, calls=%fused_computation.clone.clone.1 | custom fusion | bytes 2129920 | tf_op jit(solution)/shard_map/while/body/eval_jaxpr/jit(_take)/gather | solution.py:76
  1121.2 4.3 convolution_add_fusion.2
  1133.1 31.9 %gather_fusion = bf16[8192,64]{1,0:T(8,128)(2,1)} fusion(bf16[13825,64]{1,0:T(8,128)(2,1)S(1)} %get-tuple-element.177, s32[8192]{0:T(1024)} %broadcast_clamp_fusion.2), kind=kCustom, calls=%fused_computation.clone.clone.1 | custom fusion | bytes 2129920 | tf_op jit(solution)/shard_map/while/body/eval_jaxpr/jit(_take)/gather | solution.py:76
  1165.8 4.3 convolution_add_fusion.2
  1177.7 31.9 %gather_fusion = bf16[8192,64]{1,0:T(8,128)(2,1)} fusion(bf16[13825,64]{1,0:T(8,128)(2,1)S(1)} %get-tuple-element.177, s32[8192]{0:T(1024)} %broadcast_clamp_fusion.2), kind=kCustom, calls=%fused_computation.clone.clone.1 | custom fusion | bytes 2129920 | tf_op jit(solution)/shard_map/while/body/eval_jaxpr/jit(_take)/gather | solution.py:76
  1210.4 4.3 convolution_add_fusion.2
  1222.3 31.9 %gather_fusion = bf16[8192,64]{1,0:T(8,128)(2,1)} fusion(bf16[13825,64]{1,0:T(8,128)(2,1)S(1)} %get-tuple-element.177, s32[8192]{0:T(1024)} %broadcast_clamp_fusion.2), kind=kCustom, calls=%fused_computation.clone.clone.1 | custom fusion | bytes 2129920 | tf_op jit(solution)/shard_map/while/body/eval_jaxpr/jit(_take)/gather | solution.py:76
  1266.9 31.9 %gather_fusion = bf16[8192,64]{1,0:T(8,128)(2,1)} fusion(bf16[13825,64]{1,0:T(8,128)(2,1)S(1)} %get-tuple-element.177, s32[8192]{0:T(1024)} %broadcast_clamp_fusion.2), kind=kCustom, calls=%fused_computation.clone.clone.1 | custom fusion | bytes 2129920 | tf_op jit(solution)/shard_map/while/body/eval_jaxpr/jit(_take)/gather | solution.py:76
  1311.5 31.9 %gather_fusion = bf16[8192,64]{1,0:T(8,128)(2,1)} fusion(bf16[13825,64]{1,0:T(8,128)(2,1)S(1)} %get-tuple-element.177, s32[8192]{0:T(1024)} %broadcast_clamp_fusion.2), kind=kCustom, calls=%fused_computation.clone.clone.1 | custom fusion | bytes 2129920 | tf_op jit(solution)/shard_map/while/body/eval_jaxpr/jit(_take)/gather | solution.py:76
  1344.2 4.3 convolution_add_fusion.2
  1356.1 31.9 %gather_fusion = bf16[8192,64]{1,0:T(8,128)(2,1)} fusion(bf16[13825,64]{1,0:T(8,128)(2,1)S(1)} %get-tuple-element.177, s32[8192]{0:T(1024)} %broadcast_clamp_fusion.2), kind=kCustom, calls=%fused_computation.clone.clone.1 | custom fusion | bytes 2129920 | tf_op jit(solution)/shard_map/while/body/eval_jaxpr/jit(_take)/gather | solution.py:76
  1388.8 4.3 convolution_add_fusion.2
  1401.2 252.3 %all-reduce.3.cloned.1.call-done = f32[27,64,64]{2,1,0:T(8,128)} async-done(((f32[27,64,64]{2,1,0:T(8,128)}), f32[27,64,64]{2,1,0:T(8,128)}) %all-reduce.3.cloned.1.call-update) | async-done | bytes 442384 | tf_op jit(solution)/shard_map/psum | solution.py:88
  (416 shorter events, 362.4 us)
Async XLA Ops:
  7.2 1646.3 %all-reduce.3.cloned.1.call-start = ((), (), s32[]{:S(2)}) async-start(), calls=%async_computation | async-start | bytes 1769472 | tf_op jit(solution)/shard_map/psum | solution.py:88
  26.0 18.4 %copy-start.1 = (bf16[64,8192]{0,1:T(8,128)(2,1)S(1)}, bf16[64,8192]{0,1:T(8,128)(2,1)}, u32[]{:S(2)}) copy-start(bf16[64,8192]{0,1:T(8,128)(2,1)} %copy.9) | copy-start | bytes 3145732
  29.8 16.2 collective-permute-start
  31.1 20.1 %collective-permute-start.1 = (bf16[512,64]{1,0:T(8,128)(2,1)}, bf16[512,64]{1,0:T(8,128)(2,1)}, u32[]{:S(2)}, u32[]{:S(2)}) collective-permute-start(bf16[512,64]{1,0:T(8,128)(2,1)} %get-tuple-element.105), channel_id=1, source_target_pairs={{2,0},{4,2},{6,4},{8,6},{10,8},{12,10},{14,12},{16,14},{18,16},{20... | collective-permute-start | bytes 196616 | tf_op jit(solution)/shard_map/ppermute | solution.py:16
  32.4 21.1 %collective-permute-start.2 = (bf16[512,64]{1,0:T(8,128)(2,1)}, bf16[512,64]{1,0:T(8,128)(2,1)}, u32[]{:S(2)}, u32[]{:S(2)}) collective-permute-start(bf16[512,64]{1,0:T(8,128)(2,1)} %get-tuple-element.104), channel_id=1, source_target_pairs={{1,0},{3,2},{5,4},{7,6},{9,8},{11,10},{13,12},{15,14},{17,16},{19,... | collective-permute-start | bytes 196616 | tf_op jit(solution)/shard_map/ppermute | solution.py:16
  38.2 17.5 %collective-permute-start.3 = (bf16[512,64]{1,0:T(8,128)(2,1)}, bf16[512,64]{1,0:T(8,128)(2,1)}, u32[]{:S(2)}, u32[]{:S(2)}) collective-permute-start(bf16[512,64]{1,0:T(8,128)(2,1)} %get-tuple-element.103), channel_id=1, source_target_pairs={{0,1},{2,3},{4,5},{6,7},{8,9},{10,11},{12,13},{14,15},{16,17},{18,... | collective-permute-start | bytes 196616 | tf_op jit(solution)/shard_map/ppermute | solution.py:16
  39.5 18.4 %collective-permute-start.4 = (bf16[512,64]{1,0:T(8,128)(2,1)}, bf16[512,64]{1,0:T(8,128)(2,1)}, u32[]{:S(2)}, u32[]{:S(2)}) collective-permute-start(bf16[512,64]{1,0:T(8,128)(2,1)} %get-tuple-element.102), channel_id=1, source_target_pairs={{0,2},{2,4},{4,6},{6,8},{8,10},{10,12},{12,14},{14,16},{16,18},{18... | collective-permute-start | bytes 196616 | tf_op jit(solution)/shard_map/ppermute | solution.py:16
  46.0 15.5 collective-permute-start.5
  51.2 8.9 collective-permute-start.6
  53.5 9.4 collective-permute-start.8
  55.7 16.5 collective-permute-start.10
  58.0 19.2 %collective-permute-start.12 = (bf16[128,64]{1,0:T(8,128)(2,1)}, bf16[128,64]{1,0:T(8,128)(2,1)S(1)}, u32[]{:S(2)}, u32[]{:S(2)}) collective-permute-start(bf16[128,64]{1,0:T(8,128)(2,1)} %get-tuple-element.98), channel_id=1, source_target_pairs={{32,0},{64,32},{96,64},{128,96},{160,128},{192,160},{224,192},{33,... | collective-permute-start | bytes 49160 | tf_op jit(solution)/shard_map/ppermute | solution.py:16
  60.2 24.5 %collective-permute-start.14 = (bf16[128,64]{1,0:T(8,128)(2,1)}, bf16[128,64]{1,0:T(8,128)(2,1)S(1)}, u32[]{:S(2)}, u32[]{:S(2)}) collective-permute-start(bf16[128,64]{1,0:T(8,128)(2,1)} %get-tuple-element.97), channel_id=1, source_target_pairs={{2,0},{4,2},{6,4},{8,6},{10,8},{12,10},{14,12},{16,14},{18,16},{20... | collective-permute-start | bytes 49160 | tf_op jit(solution)/shard_map/ppermute | solution.py:16
  61.5 5.3 collective-permute-start.7
  62.8 32.0 %collective-permute-start.16 = (bf16[128,64]{1,0:T(8,128)(2,1)}, bf16[128,64]{1,0:T(8,128)(2,1)S(1)}, u32[]{:S(2)}, u32[]{:S(2)}) collective-permute-start(bf16[128,64]{1,0:T(8,128)(2,1)} %get-tuple-element.96), channel_id=1, source_target_pairs={{2,0},{4,2},{6,4},{8,6},{10,8},{12,10},{14,12},{16,14},{18,16},{20... | collective-permute-start | bytes 49160 | tf_op jit(solution)/shard_map/ppermute | solution.py:16
  66.8 9.0 collective-permute-start.9
  72.2 27.6 %collective-permute-start.18 = (bf16[128,64]{1,0:T(8,128)(2,1)}, bf16[128,64]{1,0:T(8,128)(2,1)S(1)}, u32[]{:S(2)}, u32[]{:S(2)}) collective-permute-start(bf16[128,64]{1,0:T(8,128)(2,1)} %get-tuple-element.95), channel_id=1, source_target_pairs={{0,2},{2,4},{4,6},{6,8},{8,10},{10,12},{12,14},{14,16},{16,18},{18... | collective-permute-start | bytes 49160 | tf_op jit(solution)/shard_map/ppermute | solution.py:16
  75.8 3.3 collective-permute-start.11
  77.2 30.6 %collective-permute-start.20 = (bf16[128,64]{1,0:T(8,128)(2,1)}, bf16[128,64]{1,0:T(8,128)(2,1)S(1)}, u32[]{:S(2)}, u32[]{:S(2)}) collective-permute-start(bf16[128,64]{1,0:T(8,128)(2,1)} %get-tuple-element.94), channel_id=1, source_target_pairs={{0,2},{2,4},{4,6},{6,8},{8,10},{10,12},{12,14},{14,16},{16,18},{18... | collective-permute-start | bytes 49160 | tf_op jit(solution)/shard_map/ppermute | solution.py:16
  79.1 11.8 collective-permute-start.13
  84.7 29.2 %collective-permute-start.22 = (bf16[128,64]{1,0:T(8,128)(2,1)}, bf16[128,64]{1,0:T(8,128)(2,1)S(1)}, u32[]{:S(2)}, u32[]{:S(2)}) collective-permute-start(bf16[128,64]{1,0:T(8,128)(2,1)} %get-tuple-element.93), channel_id=1, source_target_pairs={{0,32},{32,64},{64,96},{96,128},{128,160},{160,192},{192,224},{1,3... | collective-permute-start | bytes 49160 | tf_op jit(solution)/shard_map/ppermute | solution.py:16
  90.9 7.6 collective-permute-start.15
  94.8 22.2 %collective-permute-start.24 = (bf16[128,64]{1,0:T(8,128)(2,1)}, bf16[128,64]{1,0:T(8,128)(2,1)S(1)}, u32[]{:S(2)}, u32[]{:S(2)}) collective-permute-start(bf16[128,64]{1,0:T(8,128)(2,1)} %get-tuple-element.92), channel_id=1, source_target_pairs={{0,32},{32,64},{64,96},{96,128},{128,160},{160,192},{192,224},{1,3... | collective-permute-start | bytes 49160 | tf_op jit(solution)/shard_map/ppermute | solution.py:16
  98.5 5.9 collective-permute-start.17
  99.8 24.3 %collective-permute-start.26 = (bf16[128,64]{1,0:T(8,128)(2,1)}, bf16[128,64]{1,0:T(8,128)(2,1)S(1)}, u32[]{:S(2)}, u32[]{:S(2)}) collective-permute-start(bf16[128,64]{1,0:T(8,128)(2,1)} %get-tuple-element.91), channel_id=1, source_target_pairs={{0,32},{32,64},{64,96},{96,128},{128,160},{160,192},{192,224},{1,3... | collective-permute-start | bytes 49160 | tf_op jit(solution)/shard_map/ppermute | solution.py:16
  104.4 8.2 collective-permute-start.19
  107.7 19.0 %collective-permute-start.28 = (bf16[128,64]{1,0:T(8,128)(2,1)}, bf16[128,64]{1,0:T(8,128)(2,1)S(1)}, u32[]{:S(2)}, u32[]{:S(2)}) collective-permute-start(bf16[128,64]{1,0:T(8,128)(2,1)} %get-tuple-element.90), channel_id=1, source_target_pairs={{0,32},{32,64},{64,96},{96,128},{128,160},{160,192},{192,224},{1,3... | collective-permute-start | bytes 49160 | tf_op jit(solution)/shard_map/ppermute | solution.py:16
  112.6 3.1 collective-permute-start.21
  113.9 14.1 collective-permute-start.30
  115.7 5.0 collective-permute-start.23
  117.0 16.0 collective-permute-start.33
  120.7 4.7 collective-permute-start.25
  124.1 14.5 collective-permute-start.36
  125.4 6.3 collective-permute-start.27
  126.7 20.7 %collective-permute-start.39 = (bf16[128,64]{1,0:T(8,128)(2,1)}, bf16[128,64]{1,0:T(8,128)(2,1)S(1)}, u32[]{:S(2)}, u32[]{:S(2)}) collective-permute-start(bf16[128,64]{1,0:T(8,128)(2,1)} %get-tuple-element.86), channel_id=1, source_target_pairs={{32,0},{64,32},{96,64},{128,96},{160,128},{192,160},{224,192},{33,... | collective-permute-start | bytes 49160 | tf_op jit(solution)/shard_map/ppermute | solution.py:16
  128.0 14.2 collective-permute-start.29
  131.7 11.8 collective-permute-start.31
  133.0 18.1 %collective-permute-start.42 = (bf16[128,64]{1,0:T(8,128)(2,1)}, bf16[128,64]{1,0:T(8,128)(2,1)S(1)}, u32[]{:S(2)}, u32[]{:S(2)}) collective-permute-start(bf16[128,64]{1,0:T(8,128)(2,1)} %get-tuple-element.85), channel_id=1, source_target_pairs={{0,32},{32,64},{64,96},{96,128},{128,160},{160,192},{192,224},{1,3... | collective-permute-start | bytes 49160 | tf_op jit(solution)/shard_map/ppermute | solution.py:16
  138.6 17.4 %collective-permute-start.45 = (bf16[128,64]{1,0:T(8,128)(2,1)}, bf16[128,64]{1,0:T(8,128)(2,1)S(1)}, u32[]{:S(2)}, u32[]{:S(2)}) collective-permute-start(bf16[128,64]{1,0:T(8,128)(2,1)} %get-tuple-element.84), channel_id=1, source_target_pairs={{0,32},{32,64},{64,96},{96,128},{128,160},{160,192},{192,224},{1,3... | collective-permute-start | bytes 49160 | tf_op jit(solution)/shard_map/ppermute | solution.py:16
  142.2 18.7 %collective-permute-start.34 = (bf16[128,64]{1,0:T(8,128)(2,1)S(1)}, bf16[128,64]{1,0:T(8,128)(2,1)S(1)}, u32[]{:S(2)}, u32[]{:S(2)}) collective-permute-start(bf16[128,64]{1,0:T(8,128)(2,1)S(1)} %collective-permute-done.33), channel_id=1, source_target_pairs={{2,0},{4,2},{6,4},{8,6},{10,8},{12,10},{14,12},{16,14},{18,16},{20... | collective-permute-start | bytes 49160 | tf_op jit(solution)/shard_map/ppermute | solution.py:16
  143.5 21.2 %collective-permute-start.32 = (bf16[128,64]{1,0:T(8,128)(2,1)S(1)}, bf16[128,64]{1,0:T(8,128)(2,1)S(1)}, u32[]{:S(2)}, u32[]{:S(2)}) collective-permute-start(bf16[128,64]{1,0:T(8,128)(2,1)S(1)} %collective-permute-done.31), channel_id=1, source_target_pairs={{1,0},{3,2},{5,4},{7,6},{9,8},{11,10},{13,12},{15,14},{17,16},{19,... | collective-permute-start | bytes 49160 | tf_op jit(solution)/shard_map/ppermute | solution.py:16
  147.4 18.6 %collective-permute-start.48 = (bf16[128,64]{1,0:T(8,128)(2,1)}, bf16[128,64]{1,0:T(8,128)(2,1)S(1)}, u32[]{:S(2)}, u32[]{:S(2)}) collective-permute-start(bf16[128,64]{1,0:T(8,128)(2,1)} %get-tuple-element.83), channel_id=1, source_target_pairs={{0,32},{32,64},{64,96},{96,128},{128,160},{160,192},{192,224},{1,3... | collective-permute-start | bytes 49160 | tf_op jit(solution)/shard_map/ppermute | solution.py:16
  151.1 16.3 collective-permute-start.51
  156.0 12.7 collective-permute-start.37
  160.9 12.7 collective-permute-start.40
  164.8 14.6 collective-permute-start.35
  166.1 16.9 %collective-permute-start.43 = (bf16[128,64]{1,0:T(8,128)(2,1)S(1)}, bf16[128,64]{1,0:T(8,128)(2,1)S(1)}, u32[]{:S(2)}, u32[]{:S(2)}) collective-permute-start(bf16[128,64]{1,0:T(8,128)(2,1)S(1)} %collective-permute-done.42), channel_id=1, source_target_pairs={{2,0},{4,2},{6,4},{8,6},{10,8},{12,10},{14,12},{16,14},{18,16},{20... | collective-permute-start | bytes 49160 | tf_op jit(solution)/shard_map/ppermute | solution.py:16
  167.4 16.9 %collective-permute-start.46 = (bf16[128,64]{1,0:T(8,128)(2,1)S(1)}, bf16[128,64]{1,0:T(8,128)(2,1)S(1)}, u32[]{:S(2)}, u32[]{:S(2)}) collective-permute-start(bf16[128,64]{1,0:T(8,128)(2,1)S(1)} %collective-permute-done.45), channel_id=1, source_target_pairs={{2,0},{4,2},{6,4},{8,6},{10,8},{12,10},{14,12},{16,14},{18,16},{20... | collective-permute-start | bytes 49160 | tf_op jit(solution)/shard_map/ppermute | solution.py:16
  168.7 18.7 %collective-permute-start.49 = (bf16[128,64]{1,0:T(8,128)(2,1)S(1)}, bf16[128,64]{1,0:T(8,128)(2,1)S(1)}, u32[]{:S(2)}, u32[]{:S(2)}) collective-permute-start(bf16[128,64]{1,0:T(8,128)(2,1)S(1)} %collective-permute-done.48), channel_id=1, source_target_pairs={{0,2},{2,4},{4,6},{6,8},{8,10},{10,12},{12,14},{14,16},{16,18},{18... | collective-permute-start | bytes 49160 | tf_op jit(solution)/shard_map/ppermute | solution.py:16
  173.6 15.1 collective-permute-start.52
  179.4 12.3 collective-permute-start.38
  183.0 10.0 collective-permute-start.41
  184.3 8.8 collective-permute-start.44
  187.4 5.7 collective-permute-start.47
  188.7 4.4 collective-permute-start.50
  191.7 3.1 collective-permute-start.53
  407.8 4.4 copy-start
  541.6 4.4 copy-start
  586.2 4.4 copy-start
  764.5 4.4 copy-start
  898.3 4.4 copy-start
  942.9 4.4 copy-start
  1032.0 4.4 copy-start
  1165.8 4.4 copy-start
  (46 other events, 200.3 us)
Sparse Core Ops, SparseCore 0:
  1398.6 254.7 all-reduce.2
where the time goes:
time: 1690 us; the launch traced here: 1660 us
  local copies, waits for them, and re-layouts  961 us (57%)
  waiting for transfers between devices  260 us (15%)
  matrix products  185 us (11%)
  starting transfers between devices  150 us (9%)
  other arithmetic  90.5 us (5%)
    gather x27, local copies, waits for them, and re-layouts, accumulate(): picked = jnp.take(lookup_rows, indices, axis=0)  861 us
    psum x1, waiting for transfers between devices, per_device(): grad_weights = lax.psum(partial_weights, ('gx', 'gy', 'gz')) * scale_factor  252 us
    ppermute x54, starting transfers between devices, shifted(): return lax.ppermute(shard, axis, pairs)  150 us
    dot_general x27, matrix products, accumulate(): lax.dot_general(kernel, picked, (((1,), (1,)), ((), ())), preferred_eleme...  117 us
    dynamic_update_slice x54, local copies, waits for them, and re-layouts, per_device(): lax.scan(accumulate, start_sum, (weights, neighbor_map))  75.9 us
    dot_general x27, matrix products, accumulate(): partial_w = jnp.dot(features, picked, preferred_element_type=jnp.float32)  67.9 us
    select_n x27, other arithmetic, accumulate(): picked = jnp.take(lookup_rows, indices, axis=0)  43.5 us
  transfers between devices with their start and end apart: 55, of which 5 were waited for; matrix products, arithmetic and copies ran while one was open for 1% of the time, Pallas kernels for 0%

commit v1 on v0

v1 whole, which is shorter than its diff:
```python
import functools
import math

import jax
import jax.numpy as jnp
import numpy as np
from jax import lax
from jax.experimental import pallas as pl
from jax.experimental.pallas import tpu as pltpu
from jax.sharding import PartitionSpec as P

MESH = pl.DeviceIdType.MESH
AXES = ("gx", "gy", "gz")
KVOL = 27
MIDDLE = KVOL // 2
OTHERS = [k for k in range(KVOL) if k != MIDDLE]
PAIRS = len(OTHERS) // 2
TILES = 128
ROWS_MM = 2048
ROWS_BODY = 512

DIRECTIONS = [
    d
    for weight in (1, 2, 3)
    for d in [(x, y, z) for x in (-1, 0, 1) for y in (-1, 0, 1) for z in (-1, 0, 1)]
    if sum(map(abs, d)) == weight
]
CAPS = [512 if sum(map(abs, d)) == 1 else 128 for d in DIRECTIONS]
STARTS = [sum(CAPS[:j]) for j in range(len(CAPS))]
HALO = sum(CAPS)

NT = (((1,), (1,)), ((), ()))


def lane_is_low(rows):
    return lax.broadcasted_iota(jnp.int32, (rows, 128), 1) < 64


def row_masks():
    sub = lax.broadcasted_iota(jnp.int32, (8, 128), 0)
    return [sub == r for r in range(8)]


def gather_pair(table, view, consts, masks, low):
    found = [None, None]
    for q in range(4):
        here = view.at[pl.ds(q * 2, view.shape[0] - 6)]
        for side in range(2):
            for r in range(2):
                row = table[pl.ds(here[consts[side * 2 + r]], 8, stride=0), :]
                first = q == 0 and r == 0
                found[side] = (
                    row if first else jnp.where(masks[q * 2 + r], row, found[side])
                )
    return jnp.where(low, found[0], found[1])


def exchange_kernel(sizes, consts, sends, grad, table, out_rows, in_rows, send_sem, recv_sem):
    slots = grad.shape[1]
    me = [lax.axis_index(a) for a in AXES]

    def inside(sign, d):
        ok = None
        for axis in range(3):
            if d[axis] != 0:
                there = me[axis] + sign * d[axis]
                here = (there >= 0) & (there < sizes[axis])
                ok = here if ok is None else ok & here
        return ok

    def device(d):
        return tuple(me[axis] + d[axis] for axis in range(3))

    in_rows[...] = jnp.zeros_like(in_rows)
    barrier = pltpu.get_barrier_semaphore()
    for d in DIRECTIONS:

        @pl.when(inside(1, d))
        def _(d=d):
            pl.semaphore_signal(barrier, inc=1, device_id=device(d), device_id_type=MESH)

    low8, low64, masks = lane_is_low(8), lane_is_low(64), row_masks()
    one, zero = consts[1], consts[0]

    def transpose_step(b, carry):
        cols = pl.ds(pl.multiple_of(b * 128, 128), 128)
        block = grad[:, cols].astype(jnp.float32)
        table[cols, :] = jnp.concatenate([block, block], 0).T
        return carry

    lax.fori_loop(0, slots // 128, transpose_step, 0)
    table[slots : slots + 8, :] = jnp.zeros((8, 128), jnp.float32)

    def gather_unit(src, half, dst):
        cs = [zero, one, zero + half, one + half]
        view = sends.at[pl.ds(src, half + 64)]
        for t in range(4):
            parts = [
                gather_pair(table, view.at[pl.ds(t * 16 + h * 8, half + 8)], cs, masks, low8)
                for h in range(2)
            ]
            out_rows[pl.ds(pl.multiple_of(dst + t * 16, 16), 16), :] = jnp.concatenate(
                parts, 0
            ).astype(jnp.bfloat16)

    def face_unit(i, carry):
        gather_unit((i // 4) * 512 + (i % 4) * 64, 256, i * 64)
        return carry

    def edge_unit(i, carry):
        gather_unit(3072 + i * 128, 64, 1536 + i * 64)
        return carry

    def copy(j):
        rows = pl.ds(STARTS[j] // 2, CAPS[j] // 2)
        return pltpu.make_async_remote_copy(
            src_ref=out_rows.at[rows],
            dst_ref=in_rows.at[rows],
            send_sem=send_sem.at[j],
            recv_sem=recv_sem.at[j],
            device_id=device(DIRECTIONS[j]),
            device_id_type=MESH,
        )

    lax.fori_loop(0, 24, face_unit, 0)
    around = 1
    for axis in range(3):
        around *= 1 + (me[axis] > 0).astype(jnp.int32) + (me[axis] < sizes[axis] - 1).astype(jnp.int32)
    pl.semaphore_wait(barrier, around - 1)

    for j in range(6):

        @pl.when(inside(1, DIRECTIONS[j]))
        def _(j=j):
            copy(j).start()

    lax.fori_loop(0, 20, edge_unit, 0)
    for j in range(6, 26):

        @pl.when(inside(1, DIRECTIONS[j]))
        def _(j=j):
            copy(j).start()

    for j in range(26):

        @pl.when(inside(-1, DIRECTIONS[j]))
        def _(j=j):
            copy(j).wait_recv()

    def spread(src, dst, half):
        x = in_rows[pl.ds(pl.multiple_of(src, 64), 64), :].astype(jnp.float32)
        turned = pltpu.roll(x, 64, 1)
        dst = pl.multiple_of(dst, 64)
        table[pl.ds(dst, 64), :] = jnp.where(low64, x, turned)
        table[pl.ds(dst + half, 64), :] = jnp.where(low64, turned, x)

    def face_spread(i, carry):
        spread(i * 64, slots + (i // 4) * 512 + (i % 4) * 64, 256)
        return carry

    def edge_spread(i, carry):
        spread(1536 + i * 64, slots + 3072 + i * 128, 64)
        return carry

    lax.fori_loop(0, 24, face_spread, 0)
    lax.fori_loop(0, 20, edge_spread, 0)
    rest = table.shape[0] - slots - HALO
    table[slots + HALO :, :] = jnp.zeros((rest, 128), jnp.float32)

    for j in range(26):

        @pl.when(inside(1, DIRECTIONS[j]))
        def _(j=j):
            copy(j).wait_send()


def conv_kernel(consts, maps, table, grad, features, pair_weights, mid_weights, mid_map, grad_in, grad_w, total, picked):
    slots = grad.shape[1]
    p = pl.program_id(0)
    low, masks = lane_is_low(8), row_masks()
    cs = [consts[0], consts[1], consts[0] + slots, consts[1] + slots]

    @pl.when(p == 0)
    def _():
        grad_w[...] = jnp.zeros_like(grad_w)

        def middle(i, carry):
            cols = pl.ds(pl.multiple_of(i * 512, 512), 512)
            used = mid_map[:, cols] < slots
            g = jnp.where(used, grad[:, cols].astype(jnp.float32), 0.0).astype(jnp.bfloat16)
            total[:, cols] = jnp.dot(mid_weights[...], g, preferred_element_type=jnp.float32)
            grad_w[PAIRS, :, 0:64] += lax.dot_general(
                features[:, cols], g, NT, preferred_element_type=jnp.float32
            )
            return carry

        lax.fori_loop(0, slots // 512, middle, 0)

    def gather_step(j, carry):
        row = pl.multiple_of(j * ROWS_BODY, ROWS_BODY)
        view = maps.at[pl.ds(row, slots + ROWS_BODY)]
        for t in range(ROWS_BODY // 16):
            parts = [
                gather_pair(table, view.at[pl.ds(t * 16 + h * 8, slots + 8)], cs, masks, low)
                for h in range(2)
            ]
            picked[pl.ds(row + t * 16, 16), :] = jnp.concatenate(parts, 0).astype(jnp.bfloat16)
        return carry

    lax.fori_loop(0, slots // ROWS_BODY, gather_step, 0)

    def matmul_step(i, carry):
        cols = pl.ds(pl.multiple_of(i * ROWS_MM, ROWS_MM), ROWS_MM)
        rows = picked[cols, :]
        grad_w[p] += jnp.dot(features[:, cols], rows, preferred_element_type=jnp.float32)
        total[:, cols] += lax.dot_general(
            pair_weights[p], rows, NT, preferred_element_type=jnp.float32
        )
        return carry

    lax.fori_loop(0, slots // ROWS_MM, matmul_step, 0)

    @pl.when(p == PAIRS - 1)
    def _():
        def finish(i, carry):
            cols = pl.ds(pl.multiple_of(i * 512, 512), 512)
            grad_in[:, cols] = total[:, cols].astype(jnp.bfloat16)
            return carry

        lax.fori_loop(0, slots // 512, finish, 0)


def reduce_kernel(sizes, scale, terms, out, half, from_pair, from_y, from_x, back_y, whole, part, send, recv):
    nx, ny, _ = sizes
    x, y, z = [lax.axis_index(a) for a in AXES]
    own = TILES // 2
    share = own // ny

    peers_y = [lax.rem(y + s, ny) for s in range(1, ny)]
    peers_x = [lax.rem(x + s, nx) for s in range(1, nx)]
    barrier = pltpu.get_barrier_semaphore()
    targets = [(x, y, 1 - z)] + [(x, q, z) for q in peers_y] + [(q, y, z) for q in peers_x]
    for target in targets:
        pl.semaphore_signal(barrier, inc=1, device_id=target, device_id_type=MESH)
    pl.semaphore_wait(barrier, len(targets))

    def copy(src, dst, slot_send, slot_recv, target):
        return pltpu.make_async_remote_copy(
            src_ref=src,
            dst_ref=dst,
            send_sem=send.at[slot_send],
            recv_sem=recv.at[slot_recv],
            device_id=target,
            device_id_type=MESH,
        )

    first = copy(terms.at[pl.ds((1 - z) * own, own)], from_pair, 0, 0, (x, y, 1 - z))
    first.start()
    first.wait()
    half[...] = terms[pl.ds(z * own, own)] + from_pair[...]

    def to_all(base, peers, source, landing, me, place):
        sent = []
        for s, q in enumerate(peers):
            c = copy(source(q), landing(me), base + s, base + s, place(q))
            c.start()
            sent.append(c)
        return sent

    base_y = 1
    sent = to_all(
        base_y,
        peers_y,
        lambda q: half.at[pl.ds(q * share, share)],
        lambda me: from_y.at[me],
        y,
        lambda q: (x, q, z),
    )
    from_y[y] = half[pl.ds(y * share, share)]
    for c in sent:
        c.wait()
    acc = from_y[0]
    for s in range(1, ny):
        acc = acc + from_y[s]
    part[...] = acc

    base_x = base_y + ny - 1
    sent = to_all(
        base_x, peers_x, lambda q: part, lambda me: from_x.at[me], x, lambda q: (q, y, z)
    )
    from_x[x] = part[...]
    for c in sent:
        c.wait()
    acc = from_x[0]
    for s in range(1, nx):
        acc = acc + from_x[s]
    back_y[pl.ds(y * share, share)] = acc * scale

    base_b = base_x + nx - 1
    mine = back_y.at[pl.ds(y * share, share)]
    sent = to_all(base_b, peers_y, lambda q: mine, lambda me: mine, y, lambda q: (x, q, z))
    for c in sent:
        c.wait()
    last = base_b + ny - 1
    final = copy(back_y, whole.at[pl.ds(z * own, own)], last, last, (x, y, 1 - z))
    final.start()
    whole[pl.ds(z * own, own)] = back_y[...]
    final.wait()

    per = 8
    for i in range(PAIRS):
        block = whole[i * per : (i + 1) * per].reshape(64, 128)
        out[OTHERS[2 * i]] = block[:, :64]
        out[OTHERS[2 * i + 1]] = block[:, 64:]
    out[MIDDLE] = whole[PAIRS * per : (PAIRS + 1) * per].reshape(64, 128)[:, :64]


def solution(mesh):
    sizes = tuple(mesh.shape[a] for a in AXES)
    nx, ny, nz = sizes
    vmem = pl.BlockSpec(memory_space=pltpu.VMEM)
    smem = pl.BlockSpec(memory_space=pltpu.SMEM)

    def per_device(features, grad_out, weights, neighbor_map, send_list):
        slots = grad_out.shape[1]
        rows = slots + HALO + 16
        consts = jnp.arange(8, dtype=jnp.int32)
        table = pl.pallas_call(
            functools.partial(exchange_kernel, sizes),
            in_specs=[smem, smem, vmem],
            out_specs=vmem,
            out_shape=jax.ShapeDtypeStruct((rows, 128), jnp.float32),
            scratch_shapes=[
                pltpu.VMEM((HALO // 2, 128), jnp.bfloat16),
                pltpu.VMEM((HALO // 2, 128), jnp.bfloat16),
                pltpu.SemaphoreType.DMA((26,)),
                pltpu.SemaphoreType.DMA((26,)),
            ],
            compiler_params=pltpu.CompilerParams(
                collective_id=0, has_side_effects=True, vmem_limit_bytes=32 * 2**20
            ),
            name="exchange",
        )(consts, send_list, grad_out)

        maps = jnp.concatenate([neighbor_map[:MIDDLE], neighbor_map[MIDDLE + 1 :]], 0)
        others = jnp.concatenate([weights[:MIDDLE], weights[MIDDLE + 1 :]], 0)
        pair_weights = others.reshape(PAIRS, 2, 64, 64).transpose(0, 2, 1, 3).reshape(PAIRS, 64, 128)
        grad_in, terms = pl.pallas_call(
            conv_kernel,
            grid=(PAIRS,),
            in_specs=[smem, pl.BlockSpec((2 * slots,), lambda i: (i,), memory_space=pltpu.SMEM)]
            + [vmem] * 6,
            out_specs=[vmem, vmem],
            out_shape=[
                jax.ShapeDtypeStruct((64, slots), jnp.bfloat16),
                jax.ShapeDtypeStruct((TILES // 8, 64, 128), jnp.float32),
            ],
            scratch_shapes=[
                pltpu.VMEM((64, slots), jnp.float32),
                pltpu.VMEM((slots, 128), jnp.bfloat16),
            ],
            compiler_params=pltpu.CompilerParams(vmem_limit_bytes=40 * 2**20),
            name="conv",
        )(
            consts,
            maps.reshape(-1),
            table,
            grad_out,
            features,
            pair_weights,
            weights[MIDDLE],
            neighbor_map[MIDDLE : MIDDLE + 1],
        )

        own = TILES // 2
        share = own // ny
        copies = 2 + 2 * (ny - 1) + nx - 1
        tile = (8, 128)
        grad_weights = pl.pallas_call(
            functools.partial(reduce_kernel, sizes, 1.0 / math.sqrt(slots * nx * ny * nz)),
            in_specs=[vmem],
            out_specs=vmem,
            out_shape=jax.ShapeDtypeStruct((KVOL, 64, 64), jnp.float32),
            scratch_shapes=[
                pltpu.VMEM((own,) + tile, jnp.float32),
                pltpu.VMEM((own,) + tile, jnp.float32),
                pltpu.VMEM((ny, share) + tile, jnp.float32),
                pltpu.VMEM((nx, share) + tile, jnp.float32),
                pltpu.VMEM((own,) + tile, jnp.float32),
                pltpu.VMEM((TILES,) + tile, jnp.float32),
                pltpu.VMEM((share,) + tile, jnp.float32),
                pltpu.SemaphoreType.DMA((copies,)),
                pltpu.SemaphoreType.DMA((copies,)),
            ],
            compiler_params=pltpu.CompilerParams(
                collective_id=1, has_side_effects=True, vmem_limit_bytes=32 * 2**20
            ),
            name="reduce",
        )(terms.reshape((TILES,) + tile))
        return (grad_in, grad_weights)

    placed = (P(None, AXES), P(None, AXES), P(), P(None, AXES), P(AXES))
    return jax.shard_map(
        per_device,
        mesh=mesh,
        in_specs=placed,
        out_specs=(P(None, AXES), P()),
        check_vma=False,
    )
```

time: 1690 us -> 256 us (0.15); the launches traced: 1660 us -> 256 us
  local copies, waits for them, and re-layouts: 961 us -> 7.26 us
  waiting for transfers between devices: 260 us -> 0 us
  Pallas kernels: 0 us -> 246 us
  matrix products: 185 us -> 0 us
  starting transfers between devices: 150 us -> 0 us
  other arithmetic: 90.5 us -> 1.15 us
    gather x28 -> x0, local copies, waits for them, and re-layouts: 873 us -> none  [the longest x27 861 us: accumulate(): picked = jnp.take(lookup_rows, indices, axis=0)]
    psum x1 -> x0, waiting for transfers between devices: 252 us -> none  [per_device(): grad_weights = lax.psum(partial_weights, ('gx', 'gy', 'gz')) * scale_factor]
    pallas_call x0 -> x3, Pallas kernels: none -> 246 us  [the longest x1 194 us: per_device(): pl.pallas_call(conv_kernel, grid=(PAIRS,), in_specs=[smem, pl.BlockSpec((...]
    dot_general x54 -> x0, matrix products: 185 us -> none  [the longest x27 117 us: accumulate(): lax.dot_general(kernel, picked, (((1,), (1,)), ((), ())), preferred_eleme...]
    ppermute x54 -> x0, starting transfers between devices: 150 us -> none  [shifted(): return lax.ppermute(shard, axis, pairs)]
    dynamic_update_slice x54 -> x0, local copies, waits for them, and re-layouts: 75.9 us -> none  [per_device(): lax.scan(accumulate, start_sum, (weights, neighbor_map))]
    select_n x29 -> x0, other arithmetic: 47.1 us -> none  [the longest x27 43.5 us: accumulate(): picked = jnp.take(lookup_rows, indices, axis=0)]
    and x28 -> x0, other arithmetic: 21.6 us -> none  [the longest x27 20.8 us: accumulate(): picked = jnp.take(lookup_rows, indices, axis=0)]
  transfers between devices with their start and end apart: 55 -> 0, of which waited for: 5 -> 0; matrix products, arithmetic and copies ran while one was open for 1% -> 0% of each run, Pallas kernels for 0% -> 0%
where the time goes in v1:
time: 256 us
  Pallas kernels  246 us (96%)
  local copies, waits for them, and re-layouts  7.26 us (3%)
    pallas_call x1, Pallas kernels, per_device(): pl.pallas_call(conv_kernel, grid=(PAIRS,), in_specs=[smem, pl.BlockSpec((...  194 us
    pallas_call x1, Pallas kernels, per_device(): pl.pallas_call(functools.partial(reduce_kernel, sizes, 1.0 / math.sqrt(sl...  30.2 us
    pallas_call x1, Pallas kernels, per_device(): pl.pallas_call(functools.partial(exchange_kernel, sizes), in_specs=[smem,...  22.7 us

profile of v1, /device:TPU:1, one launch (start us, length us, event | category | flops | bytes accessed | tf_op | source)
XLA Modules:
  0.0 255.6 jit_solution(7093588358862042624)
XLA Ops:
  0.6 0.0 copy-start
  0.6 0.0 copy-start.2
  0.7 0.8 slice_bitcast_fusion.mid_weights
  1.5 1.0 slice.23.mid_map
  2.5 1.1 fusion.1
  3.5 0.1 pad_maximum_fusion
  3.6 0.4 copy.9
  4.1 0.2 reshape.18.pair_weights
  4.3 0.0 copy-start.1
  4.3 1.5 fusion
  5.8 1.1 pad_add_fusion
  6.8 1.4 reshape.16.maps
  8.2 0.0 copy-done
  8.2 0.0 copy-done.2
  8.2 22.7 %exchange.1.table = f32[13840,128]{1,0:T(8,128)S(1)} custom-call(s32[8]{0:T(128)S(1)} %iota.6.consts, s32[5632]{0:T(1024)S(1)} %copy-done.2, bf16[64,8192]{1,0:T(8,128)(2,1)S(1)} %copy-done), custom_call_target="tpu_custom_call" | custom-call | tf_op jit(solution)/shard_map/exchange/pallas_call | solution.py:328
  31.0 0.0 copy-done.1
  31.0 193.6 %conv.1 = (bf16[64,8192]{1,0:T(8,128)(2,1)}, f32[16,64,128]{2,1,0:T(8,128)S(1)}) custom-call(s32[8]{0:T(128)S(1)} %iota.5.consts, s32[212992]{0:T(1024)S(1)} %reshape.16.maps, f32[13840,128]{1,0:T(8,128)S(1)} %exchange.1.table, bf16[64,8192]{1,0:T(8,128)(2,1)S(1)} %copy-done, bf16[64,8192]{1,0:T(8,128)(2,1)S(1)} %copy-done.1, ...), custom_call_target="tpu_custom_call" | custom-call | tf_op jit(solution)/shard_map/conv/pallas_call | solution.py:348
  224.6 30.2 %reduce.1 = f32[27,64,64]{2,1,0:T(8,128)S(1)} custom-call(f32[128,8,128]{2,1,0:T(8,128)S(1)} %bitcast.7), custom_call_target="tpu_custom_call" | custom-call | tf_op jit(solution)/shard_map/reduce/pallas_call | solution.py:379
  254.7 0.9 copy.11
  (2 shorter events, 0.0 us)
Async XLA Ops:
  0.6 7.6 %copy-start = (bf16[64,8192]{1,0:T(8,128)(2,1)S(1)}, bf16[64,8192]{1,0:T(8,128)(2,1)}, u32[]{:S(2)}) copy-start(bf16[64,8192]{1,0:T(8,128)(2,1)} %grad.3) | copy-start | bytes 3145732
  0.6 7.6 %copy-start.2 = (s32[5632]{0:T(1024)S(1)}, s32[5632]{0:T(1024)}, u32[]{:S(2)}) copy-start(s32[5632]{0:T(1024)} %sends.1) | copy-start | bytes 67588
  4.3 26.7 %copy-start.1 = (bf16[64,8192]{1,0:T(8,128)(2,1)S(1)}, bf16[64,8192]{1,0:T(8,128)(2,1)}, u32[]{:S(2)}) copy-start(bf16[64,8192]{1,0:T(8,128)(2,1)} %features.1) | copy-start | bytes 3145732

commit v2 on v0

v2 whole, which is shorter than its diff:
```python
import functools
import math

import jax
import jax.numpy as jnp
import numpy as np
from jax import lax
from jax.experimental import pallas as pl
from jax.experimental.pallas import tpu as pltpu
from jax.sharding import PartitionSpec as P

MESH = pl.DeviceIdType.MESH
AXES = ("gx", "gy", "gz")
KVOL = 27
MIDDLE = KVOL // 2
PAIRS = MIDDLE
LATE = 2
EARLY_TILES = (PAIRS - LATE + 1) * 8
RADIX = 16
QUARTERS = 4
PIECES = (1, 8, 15, 22)
ROWS_MM = 2048
ROWS_BODY = 512

DIRECTIONS = [
    d
    for weight in (1, 2, 3)
    for d in [(x, y, z) for x in (-1, 0, 1) for y in (-1, 0, 1) for z in (-1, 0, 1)]
    if sum(map(abs, d)) == weight
]
CAPS = [512 if sum(map(abs, d)) == 1 else 128 for d in DIRECTIONS]
STARTS = [sum(CAPS[:j]) for j in range(len(CAPS))]
HALO = sum(CAPS)

NT = (((1,), (1,)), ((), ()))


def lane_is_low(rows):
    return lax.broadcasted_iota(jnp.int32, (rows, 128), 1) < 64


def row_masks():
    sub = lax.broadcasted_iota(jnp.int32, (8, 128), 0)
    return [sub == r for r in range(8)]


def gather_pair(table, pointers, at, masks, low):
    found = []
    for views in pointers:
        rows = None
        for r in range(8):
            row = table[pl.ds(views[r % 4][at + r // 4 * 4], 8, stride=0), :]
            rows = row if r == 0 else jnp.where(masks[r], row, rows)
        found.append(rows)
    return jnp.where(low, found[0], found[1])


def kernel(sizes, scale, consts, sends_in, map_a, map_b, mid_maps, grad, features_in, weights,
           grad_in, grad_w, total, staged, table, picked, whole, terms, out_rows, in_rows, halo_send, halo_recv,
           features, sends, both, early_terms, early_y, early_g, early_part, late_y, late_g, late_part,
           send, recv, load):
    slots = grad.shape[1]
    nx, ny, nz = sizes
    me = [lax.axis_index(a) for a in AXES]
    x, y, z = me
    p = pl.program_id(0)
    low, masks = lane_is_low(8), row_masks()
    shifts = [consts[r] for r in range(4)]
    mid_block = PAIRS - LATE


    def inside(sign, d):
        ok = None
        for axis in range(3):
            if d[axis] != 0:
                there = me[axis] + sign * d[axis]
                here = (there >= 0) & (there < sizes[axis])
                ok = here if ok is None else ok & here
        return ok

    def device(d):
        return tuple(me[axis] + d[axis] for axis in range(3))

    def halo_copy(j):
        rows = pl.ds(STARTS[j] // 2, CAPS[j] // 2)
        return pltpu.make_async_remote_copy(
            src_ref=out_rows.at[rows],
            dst_ref=in_rows.at[rows],
            send_sem=halo_send.at[j],
            recv_sem=halo_recv.at[j],
            device_id=device(DIRECTIONS[j]),
            device_id_type=MESH,
        )

    def transpose_step(b, carry):
        for u in range(4):
            cols = pl.ds(pl.multiple_of(b * 512 + u * 128, 128), 128)
            block = grad[:, cols].astype(jnp.float32)
            table[cols, :] = jnp.concatenate([block, block], 0).T
        return carry

    def gather_unit(src, apart, dst):
        pointers = [[sends.at[pl.ds(src + s * apart + c, 61)] for c in shifts] for s in range(2)]
        for t in range(4):
            parts = [gather_pair(table, pointers, t * 16 + h * 8, masks, low) for h in range(2)]
            out_rows[pl.ds(pl.multiple_of(dst + t * 16, 16), 16), :] = jnp.concatenate(
                parts, 0
            ).astype(jnp.bfloat16)

    def face_unit(i, carry):
        gather_unit((i // 4) * 512 + (i % 4) * 64, 256, i * 64)
        return carry

    def edge_unit(i, carry):
        gather_unit(3072 + i * 128, 64, 1536 + i * 64)
        return carry

    def middle_step(i, carry):
        cols = pl.ds(pl.multiple_of(i * 1024, 1024), 1024)
        used = mid_maps[MIDDLE % 8 : MIDDLE % 8 + 1, cols] < slots
        g = jnp.where(used, grad[:, cols].astype(jnp.float32), 0.0).astype(jnp.bfloat16)
        total[:, cols] = jnp.dot(weights[MIDDLE], g, preferred_element_type=jnp.float32)
        terms[mid_block, :, 0:64] += lax.dot_general(
            features[:, cols], g, NT, preferred_element_type=jnp.float32
        )
        return carry

    def spread(src, dst, apart):
        rows = in_rows[pl.ds(pl.multiple_of(src, 64), 64), :].astype(jnp.float32)
        turned = pltpu.roll(rows, 64, 1)
        dst = pl.multiple_of(dst, 64)
        low64 = lane_is_low(64)
        table[pl.ds(dst, 64), :] = jnp.where(low64, rows, turned)
        table[pl.ds(dst + apart, 64), :] = jnp.where(low64, turned, rows)

    def face_spread(i, carry):
        spread(i * 64, slots + (i // 4) * 512 + (i % 4) * 64, 256)
        return carry

    def edge_spread(i, carry):
        spread(1536 + i * 64, slots + 3072 + i * 128, 64)
        return carry

    digits = [y, x * nz + z]

    def member(group, q):
        return (x, q, z) if group == 0 else (q // nz, y, lax.rem(q, nz))

    def others(group):
        return [lax.rem(digits[group] + s, RADIX) for s in range(1, RADIX)]

    load_features = pltpu.make_async_copy(features_in, features, load.at[0])
    load_sends = pltpu.make_async_copy(sends_in, sends, load.at[1])
    store_in = pltpu.make_async_copy(staged, grad_in, load.at[2])

    @pl.when(p == 0)
    def _():
        load_sends.start()
        load_features.start()
        in_rows[...] = jnp.zeros_like(in_rows)
        barrier = pltpu.get_barrier_semaphore()
        for d in DIRECTIONS:

            @pl.when(inside(1, d))
            def _(d=d):
                pl.semaphore_signal(barrier, inc=1, device_id=device(d), device_id_type=MESH)

        for group in range(2):
            for q in others(group):
                pl.semaphore_signal(
                    barrier, inc=1, device_id=member(group, q), device_id_type=MESH
                )
        terms[...] = jnp.zeros_like(terms)
        picked[slots // ROWS_BODY - 1] = jnp.zeros(picked.shape[1:], picked.dtype)
        for i in range(PAIRS):
            both[i] = jnp.concatenate([weights[i], weights[i + MIDDLE + 1]], 1)

        lax.fori_loop(0, slots // 512, transpose_step, 0)
        table[slots : slots + 8, :] = jnp.zeros((8, 128), jnp.float32)
        load_sends.wait()
        lax.fori_loop(0, 24, face_unit, 0)

        around = 1
        for axis in range(3):
            around *= (
                1
                + (me[axis] > 0).astype(jnp.int32)
                + (me[axis] < sizes[axis] - 1).astype(jnp.int32)
            )
        pl.semaphore_wait(barrier, around - 1 + 2 * (RADIX - 1))

        def start(j):
            @pl.when(inside(1, DIRECTIONS[j]))
            def _():
                halo_copy(j).start()

        for j in range(6):
            start(j)
        lax.fori_loop(0, 20, edge_unit, 0)
        for j in range(6, 26):
            start(j)

        load_features.wait()
        lax.fori_loop(0, slots // 1024, middle_step, 0)

        for j in range(26):

            @pl.when(inside(-1, DIRECTIONS[j]))
            def _(j=j):
                halo_copy(j).wait_recv()

        lax.fori_loop(0, 24, face_spread, 0)
        lax.fori_loop(0, 20, edge_spread, 0)
        rest = table.shape[0] - slots - HALO
        table[slots + HALO :, :] = jnp.zeros((rest, 128), jnp.float32)

        for j in range(26):

            @pl.when(inside(1, DIRECTIONS[j]))
            def _(j=j):
                halo_copy(j).wait_send()


    terms_tiles = terms.reshape(terms.shape[0] * 8, 8, 128)

    def exchange(slot, group, source, landing):
        return [
            pltpu.make_async_remote_copy(
                src_ref=source(q),
                dst_ref=landing(digits[group]),
                send_sem=send.at[slot * (RADIX - 1) + s],
                recv_sem=recv.at[slot * (RADIX - 1) + s],
                device_id=member(group, q),
                device_id_type=MESH,
            )
            for s, q in enumerate(others(group))
        ]

    def start_all(copies):
        for c in copies:
            c.start()

    def wait_recv(copies):
        for c in copies:
            c.wait_recv()

    def wait_send(copies):
        for c in copies:
            c.wait_send()

    def added(ref):
        acc = ref[0]
        for s in range(1, RADIX):
            acc = acc + ref[s]
        return acc

    def summation(slot, source, first, base, count, in_y, in_g, part):
        mine = pl.ds(base + y * count, count)
        phases = [
            exchange(slot, 0, lambda q: source.at[pl.ds(first + q * count, count)], lambda d: in_y.at[d]),
            exchange(slot + 1, 1, lambda q: part, lambda d: in_g.at[d]),
            exchange(slot + 2, 0, lambda q: whole.at[mine], lambda d: whole.at[mine]),
        ]

        def step(n):
            if n > 0:
                wait_recv(phases[n - 1])
            if n == 0:
                start_all(phases[0])
                in_y[y] = source[pl.ds(first + y * count, count)]
            elif n == 1:
                part[...] = added(in_y)
                start_all(phases[1])
                in_g[digits[1]] = part[...]
            elif n == 2:
                whole[mine] = added(in_g) * scale
                start_all(phases[2])
            elif n == 3:
                for copies in phases:
                    wait_send(copies)

        return step

    early_step = summation(
        0, early_terms, 0, 0, EARLY_TILES // RADIX, early_y, early_g, early_part
    )
    late_step = summation(
        3, terms_tiles, EARLY_TILES, EARLY_TILES, LATE * 8 // RADIX, late_y, late_g, late_part
    )

    def reduce_step(quarter):
        for n, at in enumerate((1, 3, 6)):

            @pl.when((p - (PAIRS - 2)) * QUARTERS + quarter == at)
            def _(n=n):
                if n == 0:
                    early_terms[...] = terms_tiles[0:EARLY_TILES]
                early_step(n)


    steps = slots // ROWS_BODY

    def matmul_piece(pair, j, piece):
        count = ROWS_BODY * 2 // len(PIECES)
        first = piece // 2 * count
        cols = pl.ds(pl.multiple_of(j * ROWS_BODY + first, count), count)
        rows = picked[j, first : first + count, :]
        if piece % 2 == 0:
            block = jnp.where(pair < mid_block, pair, pair + 1)
            terms[block] += jnp.dot(features[:, cols], rows, preferred_element_type=jnp.float32)
        else:
            total[:, cols] += lax.dot_general(
                both[pair], rows, NT, preferred_element_type=jnp.float32
            )

    def gather_step(j, carry):
        before = p * steps + j - 1
        pair_before = jnp.maximum(before, 0) // steps
        step_before = lax.rem(before + steps, steps)
        row = pl.multiple_of(j * ROWS_BODY, ROWS_BODY)
        pointers = [[m.at[pl.ds(row + c, ROWS_BODY - 3)] for c in shifts] for m in (map_a, map_b)]
        for t in range(ROWS_BODY // 16):
            if t in PIECES:
                matmul_piece(pair_before, step_before, PIECES.index(t))
            parts = [gather_pair(table, pointers, t * 16 + h * 8, masks, low) for h in range(2)]
            picked[j, t * 16 : (t + 1) * 16, :] = jnp.concatenate(parts, 0).astype(jnp.bfloat16)
        return carry

    def gather_quarter(quarter, carry):
        @pl.when(p >= PAIRS - 2)
        def _():
            reduce_step(quarter)

        some = steps // QUARTERS
        return lax.fori_loop(quarter * some, (quarter + 1) * some, gather_step, carry)

    lax.fori_loop(0, QUARTERS, gather_quarter, 0)

    @pl.when(p == PAIRS - 1)
    def _():
        for piece in range(len(PIECES)):
            matmul_piece(PAIRS - 1, steps - 1, piece)

        def put(block, first, last):
            found = whole[pl.ds(block * 8, 8)].reshape(64, 128)
            if first is not None:
                grad_w[first] = found[:, :64]
            if last is not None:
                grad_w[last] = found[:, 64:]

        late_step(0)

        def finish(i, carry):
            cols = pl.ds(pl.multiple_of(i * 1024, 1024), 1024)
            staged[:, cols] = total[:, cols].astype(jnp.bfloat16)
            return carry

        lax.fori_loop(0, slots // 1024, finish, 0)
        store_in.start()
        early_step(3)
        late_step(1)
        for i in range(PAIRS - LATE):
            put(i, i, i + MIDDLE + 1)
        put(mid_block, MIDDLE, None)
        late_step(2)
        late_step(3)
        for i in range(PAIRS - LATE, PAIRS):
            put(i + 1, i, i + MIDDLE + 1)
        store_in.wait()


def solution(mesh):
    sizes = tuple(mesh.shape[a] for a in AXES)
    nx, ny, nz = sizes
    vmem = pl.BlockSpec(memory_space=pltpu.VMEM)
    smem = pl.BlockSpec(memory_space=pltpu.SMEM)

    def per_device(features, grad_out, weights, neighbor_map, send_list):
        slots = grad_out.shape[1]
        consts = jnp.arange(4, dtype=jnp.int32)
        maps = neighbor_map.reshape(-1)
        early_share = EARLY_TILES // RADIX
        late_share = LATE * 8 // RADIX
        all_tiles = EARLY_TILES + LATE * 8
        copies = 6 * (RADIX - 1)
        anywhere = pl.BlockSpec(memory_space=pl.ANY)
        f32, bf16 = jnp.float32, jnp.bfloat16

        def tiled(*lead):
            return pltpu.VMEM(lead + (8, 128), f32)

        grad_in, grad_weights = pl.pallas_call(
            functools.partial(kernel, sizes, 1.0 / math.sqrt(slots * nx * ny * nz)),
            grid=(PAIRS,),
            in_specs=[
                smem,
                anywhere,
                pl.BlockSpec((slots,), lambda i: (i,), memory_space=pltpu.SMEM),
                pl.BlockSpec((slots,), lambda i: (i + MIDDLE + 1,), memory_space=pltpu.SMEM),
                pl.BlockSpec((8, slots), lambda i: (MIDDLE // 8, 0)),
                vmem,
                anywhere,
                vmem,
            ],
            out_specs=[anywhere, vmem],
            out_shape=[
                jax.ShapeDtypeStruct((64, slots), bf16),
                jax.ShapeDtypeStruct((KVOL, 64, 64), f32),
            ],
            scratch_shapes=[
                pltpu.VMEM((64, slots), f32),
                pltpu.VMEM((64, slots), bf16),
                pltpu.VMEM((slots + HALO + 16, 128), f32),
                pltpu.VMEM((slots // ROWS_BODY, ROWS_BODY, 128), bf16),
                tiled(all_tiles),
                pltpu.VMEM((all_tiles // 8, 64, 128), f32),
                pltpu.VMEM((HALO // 2, 128), bf16),
                pltpu.VMEM((HALO // 2, 128), bf16),
                pltpu.SemaphoreType.DMA((26,)),
                pltpu.SemaphoreType.DMA((26,)),
                pltpu.VMEM((64, slots), bf16),
                pltpu.SMEM((HALO,), jnp.int32),
                pltpu.VMEM((PAIRS, 64, 128), bf16),
                tiled(EARLY_TILES),
                tiled(RADIX, early_share),
                tiled(RADIX, early_share),
                tiled(early_share),
                tiled(RADIX, late_share),
                tiled(RADIX, late_share),
                tiled(late_share),
                pltpu.SemaphoreType.DMA((copies,)),
                pltpu.SemaphoreType.DMA((copies,)),
                pltpu.SemaphoreType.DMA((3,)),
            ],
            compiler_params=pltpu.CompilerParams(
                collective_id=0, has_side_effects=True, vmem_limit_bytes=62 * 2**20
            ),
            name="conv",
        )(consts, send_list, maps, maps, neighbor_map, grad_out, features, weights)

        return (grad_in, grad_weights)

    placed = (P(None, AXES), P(None, AXES), P(), P(None, AXES), P(AXES))
    return jax.shard_map(
        per_device,
        mesh=mesh,
        in_specs=placed,
        out_specs=(P(None, AXES), P()),
        check_vma=False,
    )
```

time: 1690 us -> 197 us (0.12); the launches traced: 1660 us -> 197 us
  local copies, waits for them, and re-layouts: 961 us -> 6.06 us
  waiting for transfers between devices: 260 us -> 0 us
  Pallas kernels: 0 us -> 190 us
  matrix products: 185 us -> 0 us
  starting transfers between devices: 150 us -> 0 us
  other arithmetic: 90.5 us -> 0 us
    gather x28 -> x0, local copies, waits for them, and re-layouts: 873 us -> none  [the longest x27 861 us: accumulate(): picked = jnp.take(lookup_rows, indices, axis=0)]
    psum x1 -> x0, waiting for transfers between devices: 252 us -> none  [per_device(): grad_weights = lax.psum(partial_weights, ('gx', 'gy', 'gz')) * scale_factor]
    pallas_call x0 -> x1, Pallas kernels: none -> 190 us  [per_device(): pl.pallas_call(functools.partial(kernel, sizes, 1.0 / math.sqrt(slots * n...]
    dot_general x54 -> x0, matrix products: 185 us -> none  [the longest x27 117 us: accumulate(): lax.dot_general(kernel, picked, (((1,), (1,)), ((), ())), preferred_eleme...]
    ppermute x54 -> x0, starting transfers between devices: 150 us -> none  [shifted(): return lax.ppermute(shard, axis, pairs)]
    dynamic_update_slice x54 -> x0, local copies, waits for them, and re-layouts: 75.9 us -> none  [per_device(): lax.scan(accumulate, start_sum, (weights, neighbor_map))]
    select_n x29 -> x0, other arithmetic: 47.1 us -> none  [the longest x27 43.5 us: accumulate(): picked = jnp.take(lookup_rows, indices, axis=0)]
    and x28 -> x0, other arithmetic: 21.6 us -> none  [the longest x27 20.8 us: accumulate(): picked = jnp.take(lookup_rows, indices, axis=0)]
  transfers between devices with their start and end apart: 55 -> 0, of which waited for: 5 -> 0; matrix products, arithmetic and copies ran while one was open for 1% -> 0% of each run, Pallas kernels for 0% -> 0%
where the time goes in v2:
time: 197 us
  Pallas kernels  190 us (96%)
  local copies, waits for them, and re-layouts  6.06 us (3%)
    pallas_call x1, Pallas kernels, per_device(): pl.pallas_call(functools.partial(kernel, sizes, 1.0 / math.sqrt(slots * n...  190 us

profile of v2, /device:TPU:1, one launch (start us, length us, event | category | flops | bytes accessed | tf_op | source)
XLA Modules:
  0.0 196.8 jit_solution(2031224839737663805)
XLA Ops:
  0.6 0.5 iota.3.consts
  1.1 2.3 %reshape.7.map_a.map_b = s32[221184]{0:T(1024)} reshape(s32[27,8192]{1,0:T(8,128)} %mid_maps.1) | data formatting | bytes 1769472 | tf_op jit(solution)/shard_map/reshape | solution.py:381
  3.4 190.1 %conv.1 = (bf16[64,8192]{1,0:T(8,128)(2,1)}, f32[27,64,64]{2,1,0:T(8,128)}) custom-call(s32[4]{0:T(128)} %iota.3.consts, s32[5632]{0:T(1024)} %sends_in.1, s32[221184]{0:T(1024)} %reshape.7.map_a.map_b, s32[221184]{0:T(1024)} %reshape.7.map_a.map_b, s32[27,8192]{1,0:T(8,128)} %mid_maps.1, bf16[64,8192]{1,0:T(8,128)(2,1)} %grad.1, ...), custom_call_target="tpu_custom_call" | custom-call | tf_op jit(solution)/shard_map/conv/pallas_call | solution.py:392
  193.6 0.0 copy-start
  193.6 2.3 %copy.9 = bf16[64,8192]{1,0:T(8,128)(2,1)} copy(bf16[64,8192]{1,0:T(8,128)(2,1)} %get-tuple-element.4) | data formatting | bytes 2097152
  195.9 0.0 copy-done
  195.9 0.9 copy.10
Async XLA Ops:
  193.6 2.4 %copy-start = (f32[27,64,64]{2,1,0:T(8,128)S(1)}, f32[27,64,64]{2,1,0:T(8,128)}, u32[]{:S(2)}) copy-start(f32[27,64,64]{2,1,0:T(8,128)} %get-tuple-element.5) | copy-start | bytes 1327108

commit v3 on v2

--- a/solution.py
+++ b/solution.py
@@ -18,9 +18,9 @@
 EARLY_TILES = (PAIRS - LATE + 1) * 8
 RADIX = 16
 QUARTERS = 4
-PIECES = (1, 8, 15, 22)
+PIECES = (2, 8, 14, 20, 26, 32, 38, 44)
 ROWS_MM = 2048
-ROWS_BODY = 512
+ROWS_BODY = 1024
 
 DIRECTIONS = [
     d
@@ -55,17 +55,26 @@
     return jnp.where(low, found[0], found[1])
 
 
-def kernel(sizes, scale, consts, sends_in, map_a, map_b, mid_maps, grad, features_in, weights,
-           grad_in, grad_w, total, staged, table, picked, whole, terms, out_rows, in_rows, halo_send, halo_recv,
+def kernel(sizes, scale, sends_in, maps, mid_maps, grad, features_in, weights,
+           grad_in, grad_w, total, table, picked, whole, terms, out_rows, in_rows, halo_send, halo_recv,
            features, sends, both, early_terms, early_y, early_g, early_part, late_y, late_g, late_part,
-           send, recv, load):
+           send, recv, load, lists):
     slots = grad.shape[1]
     nx, ny, nz = sizes
     me = [lax.axis_index(a) for a in AXES]
     x, y, z = me
     p = pl.program_id(0)
     low, masks = lane_is_low(8), row_masks()
-    shifts = [consts[r] for r in range(4)]
+    shifts = [(r * nx + x) // nx for r in range(4)]
+
+    def load_list(pair, side):
+        slot = lax.rem(pair, 2) * 2 + side
+        return pltpu.make_async_copy(
+            maps.at[pair + side * (MIDDLE + 1)],
+            lists.at[pl.ds(slot * slots, slots)],
+            load.at[3 + slot],
+        )
+
     mid_block = PAIRS - LATE
 
 
@@ -151,12 +160,14 @@
 
     load_features = pltpu.make_async_copy(features_in, features, load.at[0])
     load_sends = pltpu.make_async_copy(sends_in, sends, load.at[1])
-    store_in = pltpu.make_async_copy(staged, grad_in, load.at[2])
+    store_in = pltpu.make_async_copy(total, grad_in, load.at[2])
 
     @pl.when(p == 0)
     def _():
         load_sends.start()
         load_features.start()
+        for side in range(2):
+            load_list(0, side).start()
         in_rows[...] = jnp.zeros_like(in_rows)
         barrier = pltpu.get_barrier_semaphore()
         for d in DIRECTIONS:
@@ -170,16 +181,15 @@
                 pl.semaphore_signal(
                     barrier, inc=1, device_id=member(group, q), device_id_type=MESH
                 )
-        terms[...] = jnp.zeros_like(terms)
-        picked[slots // ROWS_BODY - 1] = jnp.zeros(picked.shape[1:], picked.dtype)
-        for i in range(PAIRS):
-            both[i] = jnp.concatenate([weights[i], weights[i + MIDDLE + 1]], 1)
 
         lax.fori_loop(0, slots // 512, transpose_step, 0)
         table[slots : slots + 8, :] = jnp.zeros((8, 128), jnp.float32)
+        def start(j):
+            @pl.when(inside(1, DIRECTIONS[j]))
+            def _():
+                halo_copy(j).start()
+
         load_sends.wait()
-        lax.fori_loop(0, 24, face_unit, 0)
-
         around = 1
         for axis in range(3):
             around *= (
@@ -187,19 +197,22 @@
                 + (me[axis] > 0).astype(jnp.int32)
                 + (me[axis] < sizes[axis] - 1).astype(jnp.int32)
             )
-        pl.semaphore_wait(barrier, around - 1 + 2 * (RADIX - 1))
-
-        def start(j):
-            @pl.when(inside(1, DIRECTIONS[j]))
-            def _():
-                halo_copy(j).start()
-
         for j in range(6):
-            start(j)
+            lax.fori_loop(4 * j, 4 * j + 4, face_unit, 0)
+            if j == 2:
+                pl.semaphore_wait(barrier, around - 1 + 2 * (RADIX - 1))
+                for k in range(2):
+                    start(k)
+            if j >= 2:
+                start(j)
         lax.fori_loop(0, 20, edge_unit, 0)
         for j in range(6, 26):
             start(j)
 
+        terms[...] = jnp.zeros_like(terms)
+        picked[slots // ROWS_BODY - 1] = jnp.zeros(picked.shape[1:], picked.dtype)
+        for i in range(PAIRS):
+            both[i] = jnp.concatenate([weights[i], weights[i + MIDDLE + 1]], 1)
         load_features.wait()
         lax.fori_loop(0, slots // 1024, middle_step, 0)
 
@@ -318,13 +331,25 @@
         pair_before = jnp.maximum(before, 0) // steps
         step_before = lax.rem(before + steps, steps)
         row = pl.multiple_of(j * ROWS_BODY, ROWS_BODY)
-        pointers = [[m.at[pl.ds(row + c, ROWS_BODY - 3)] for c in shifts] for m in (map_a, map_b)]
+        slot = lax.rem(p, 2) * 2
+        pointers = [
+            [lists.at[pl.ds((slot + side) * slots + row + c, ROWS_BODY - 3)] for c in shifts]
+            for side in range(2)
+        ]
         for t in range(ROWS_BODY // 16):
             if t in PIECES:
                 matmul_piece(pair_before, step_before, PIECES.index(t))
             parts = [gather_pair(table, pointers, t * 16 + h * 8, masks, low) for h in range(2)]
             picked[j, t * 16 : (t + 1) * 16, :] = jnp.concatenate(parts, 0).astype(jnp.bfloat16)
         return carry
+
+    for side in range(2):
+        load_list(p, side).wait()
+
+    @pl.when(p < PAIRS - 1)
+    def _():
+        for side in range(2):
+            load_list(p + 1, side).start()
 
     def gather_quarter(quarter, carry):
         @pl.when(p >= PAIRS - 2)
@@ -350,12 +375,6 @@
 
         late_step(0)
 
-        def finish(i, carry):
-            cols = pl.ds(pl.multiple_of(i * 1024, 1024), 1024)
-            staged[:, cols] = total[:, cols].astype(jnp.bfloat16)
-            return carry
-
-        lax.fori_loop(0, slots // 1024, finish, 0)
         store_in.start()
         early_step(3)
         late_step(1)
@@ -377,8 +396,6 @@
 
     def per_device(features, grad_out, weights, neighbor_map, send_list):
         slots = grad_out.shape[1]
-        consts = jnp.arange(4, dtype=jnp.int32)
-        maps = neighbor_map.reshape(-1)
         early_share = EARLY_TILES // RADIX
         late_share = LATE * 8 // RADIX
         all_tiles = EARLY_TILES + LATE * 8
@@ -393,10 +410,8 @@
             functools.partial(kernel, sizes, 1.0 / math.sqrt(slots * nx * ny * nz)),
             grid=(PAIRS,),
             in_specs=[
-                smem,
                 anywhere,
-                pl.BlockSpec((slots,), lambda i: (i,), memory_space=pltpu.SMEM),
-                pl.BlockSpec((slots,), lambda i: (i + MIDDLE + 1,), memory_space=pltpu.SMEM),
+                anywhere,
                 pl.BlockSpec((8, slots), lambda i: (MIDDLE // 8, 0)),
                 vmem,
                 anywhere,
@@ -404,12 +419,11 @@
             ],
             out_specs=[anywhere, vmem],
             out_shape=[
-                jax.ShapeDtypeStruct((64, slots), bf16),
+                jax.ShapeDtypeStruct((64, slots), f32),
                 jax.ShapeDtypeStruct((KVOL, 64, 64), f32),
             ],
             scratch_shapes=[
                 pltpu.VMEM((64, slots), f32),
-                pltpu.VMEM((64, slots), bf16),
                 pltpu.VMEM((slots + HALO + 16, 128), f32),
                 pltpu.VMEM((slots // ROWS_BODY, ROWS_BODY, 128), bf16),
                 tiled(all_tiles),
@@ -430,15 +444,16 @@
                 tiled(late_share),
                 pltpu.SemaphoreType.DMA((copies,)),
                 pltpu.SemaphoreType.DMA((copies,)),
-                pltpu.SemaphoreType.DMA((3,)),
+                pltpu.SemaphoreType.DMA((7,)),
+                pltpu.SMEM((4 * slots,), jnp.int32),
             ],
             compiler_params=pltpu.CompilerParams(
                 collective_id=0, has_side_effects=True, vmem_limit_bytes=62 * 2**20
             ),
             name="conv",
-        )(consts, send_list, maps, maps, neighbor_map, grad_out, features, weights)
-
-        return (grad_in, grad_weights)
+        )(send_list, neighbor_map, neighbor_map, grad_out, features, weights)
+
+        return (grad_in.astype(bf16), grad_weights)
 
     placed = (P(None, AXES), P(None, AXES), P(), P(None, AXES), P(AXES))
     return jax.shard_map(

time: 197 us -> 195 us (0.990)
  local copies, waits for them, and re-layouts: 6.06 us -> 0.92 us
  other arithmetic: 0 us -> 2.74 us
    convert_element_type x0 -> x1, other arithmetic: none -> 2.74 us  [per_device(): return (grad_in.astype(bf16), grad_weights)]
    unnamed x4 -> x3, local copies, waits for them, and re-layouts: 3.26 us -> 0.92 us
    reshape x1 -> x0, local copies, waits for them, and re-layouts: 2.29 us -> none  [per_device(): maps = neighbor_map.reshape(-1)]
where the time goes in v3:
time: 195 us
  Pallas kernels  190 us (97%)
  other arithmetic  2.74 us (1%)
    pallas_call x1, Pallas kernels, per_device(): pl.pallas_call(functools.partial(kernel, sizes, 1.0 / math.sqrt(slots * n...  190 us

profile of v3, /device:TPU:1, one launch (start us, length us, event | category | flops | bytes accessed | tf_op | source)
XLA Modules:
  0.0 194.5 jit_solution(12006305178382112178)
XLA Ops:
  0.6 190.2 %conv.1 = (f32[64,8192]{1,0:T(8,128)}, f32[27,64,64]{2,1,0:T(8,128)}) custom-call(s32[5632]{0:T(1024)} %sends_in.1, s32[27,8192]{1,0:T(8,128)} %mid_maps.1, s32[27,8192]{1,0:T(8,128)} %mid_maps.1, bf16[64,8192]{1,0:T(8,128)(2,1)} %grad.1, bf16[64,8192]{1,0:T(8,128)(2,1)} %features_in.1, bf16[27,64,64]{2,1,0:T(8,128)(2,1)} %weights.1), custom_call_target="tpu_custom_call" | custom-call | tf_op jit(solution)/shard_map/conv/pallas_call | solution.py:409
  190.8 0.0 copy-start
  190.8 2.7 %convert_element_type.3 = bf16[64,8192]{1,0:T(8,128)(2,1)} convert(f32[64,8192]{1,0:T(8,128)} %get-tuple-element.4) | non-fusion elementwise | flops 524288 | bytes 3145728 | tf_op jit(solution)/shard_map/convert_element_type | solution.py:456
  193.6 0.0 copy-done
  193.6 0.9 copy.8
Async XLA Ops:
  190.8 2.8 %copy-start = (f32[27,64,64]{2,1,0:T(8,128)S(1)}, f32[27,64,64]{2,1,0:T(8,128)}, u32[]{:S(2)}) copy-start(f32[27,64,64]{2,1,0:T(8,128)} %get-tuple-element.9) | copy-start | bytes 1327108

commit v4 on v3

--- a/solution.py
+++ b/solution.py
@@ -14,7 +14,7 @@
 KVOL = 27
 MIDDLE = KVOL // 2
 PAIRS = MIDDLE
-LATE = 2
+LATE = 4
 EARLY_TILES = (PAIRS - LATE + 1) * 8
 RADIX = 16
 QUARTERS = 4
@@ -56,7 +56,7 @@
 
 
 def kernel(sizes, scale, sends_in, maps, mid_maps, grad, features_in, weights,
-           grad_in, grad_w, total, table, picked, whole, terms, out_rows, in_rows, halo_send, halo_recv,
+           grad_in, grad_w, total, staged, table, picked, whole, terms, out_rows, in_rows, halo_send, halo_recv,
            features, sends, both, early_terms, early_y, early_g, early_part, late_y, late_g, late_part,
            send, recv, load, lists):
     slots = grad.shape[1]
@@ -160,7 +160,7 @@
 
     load_features = pltpu.make_async_copy(features_in, features, load.at[0])
     load_sends = pltpu.make_async_copy(sends_in, sends, load.at[1])
-    store_in = pltpu.make_async_copy(total, grad_in, load.at[2])
+    store_in = pltpu.make_async_copy(staged, grad_in, load.at[2])
 
     @pl.when(p == 0)
     def _():
@@ -302,9 +302,9 @@
     )
 
     def reduce_step(quarter):
-        for n, at in enumerate((1, 3, 6)):
-
-            @pl.when((p - (PAIRS - 2)) * QUARTERS + quarter == at)
+        for n, at in enumerate((1, 5, 10)):
+
+            @pl.when((p - (PAIRS - LATE)) * QUARTERS + quarter == at)
             def _(n=n):
                 if n == 0:
                     early_terms[...] = terms_tiles[0:EARLY_TILES]
@@ -352,7 +352,7 @@
             load_list(p + 1, side).start()
 
     def gather_quarter(quarter, carry):
-        @pl.when(p >= PAIRS - 2)
+        @pl.when(p >= PAIRS - LATE)
         def _():
             reduce_step(quarter)
 
@@ -375,6 +375,12 @@
 
         late_step(0)
 
+        def finish(i, carry):
+            cols = pl.ds(pl.multiple_of(i * 1024, 1024), 1024)
+            staged[:, cols] = total[:, cols].astype(jnp.bfloat16)
+            return carry
+
+        lax.fori_loop(0, slots // 1024, finish, 0)
         store_in.start()
         early_step(3)
         late_step(1)
@@ -419,11 +425,12 @@
             ],
             out_specs=[anywhere, vmem],
             out_shape=[
-                jax.ShapeDtypeStruct((64, slots), f32),
+                jax.ShapeDtypeStruct((64, slots), bf16),
                 jax.ShapeDtypeStruct((KVOL, 64, 64), f32),
             ],
             scratch_shapes=[
                 pltpu.VMEM((64, slots), f32),
+                pltpu.VMEM((64, slots), bf16),
                 pltpu.VMEM((slots + HALO + 16, 128), f32),
                 pltpu.VMEM((slots // ROWS_BODY, ROWS_BODY, 128), bf16),
                 tiled(all_tiles),
@@ -453,7 +460,7 @@
             name="conv",
         )(send_list, neighbor_map, neighbor_map, grad_out, features, weights)
 
-        return (grad_in.astype(bf16), grad_weights)
+        return (grad_in, grad_weights)
 
     placed = (P(None, AXES), P(None, AXES), P(), P(None, AXES), P(AXES))
     return jax.shard_map(

time: 195 us -> 192 us (0.985)
  other arithmetic: 2.74 us -> 0 us
  local copies, waits for them, and re-layouts: 0.92 us -> 3.26 us
  Pallas kernels: 190 us -> 188 us
    convert_element_type x1 -> x0, other arithmetic: 2.74 us -> none  [per_device(): return (grad_in.astype(bf16), grad_weights)]
    unnamed x3 -> x4, local copies, waits for them, and re-layouts: 0.92 us -> 3.26 us
where the time goes in v4:
time: 192 us
  Pallas kernels  188 us (98%)
  local copies, waits for them, and re-layouts  3.26 us (2%)
    pallas_call x1, Pallas kernels, per_device(): pl.pallas_call(functools.partial(kernel, sizes, 1.0 / math.sqrt(slots * n...  188 us

profile of v4, /device:TPU:1, one launch (start us, length us, event | category | flops | bytes accessed | tf_op | source)
XLA Modules:
  0.0 192.3 jit_solution(13704670912138263095)
XLA Ops:
  0.6 188.4 %conv.1 = (bf16[64,8192]{1,0:T(8,128)(2,1)}, f32[27,64,64]{2,1,0:T(8,128)}) custom-call(s32[5632]{0:T(1024)} %sends_in.1, s32[27,8192]{1,0:T(8,128)} %mid_maps.1, s32[27,8192]{1,0:T(8,128)} %mid_maps.1, bf16[64,8192]{1,0:T(8,128)(2,1)} %grad.1, bf16[64,8192]{1,0:T(8,128)(2,1)} %features_in.1, bf16[27,64,64]{2,1,0:T(8,128)(2,1)} %weights.1), custom_call_target="tpu_custom_call" | custom-call | tf_op jit(solution)/shard_map/conv/pallas_call | solution.py:415
  189.0 0.0 copy-start
  189.0 2.3 %copy.9 = bf16[64,8192]{1,0:T(8,128)(2,1)} copy(bf16[64,8192]{1,0:T(8,128)(2,1)} %get-tuple-element.4) | data formatting | bytes 2097152
  191.4 0.0 copy-done
  191.4 0.9 copy.10
Async XLA Ops:
  189.0 2.4 %copy-start = (f32[27,64,64]{2,1,0:T(8,128)S(1)}, f32[27,64,64]{2,1,0:T(8,128)}, u32[]{:S(2)}) copy-start(f32[27,64,64]{2,1,0:T(8,128)} %get-tuple-element.5) | copy-start | bytes 1327108
